TPU v7x, 32 devices: a whole 2x2x4 slice. The times are simulated.
32 devices in a mesh: rep: 2 (over y), ada: 16 (over z, x, core).
Axes of the slice: x: 2, y: 2, z: 4, core: 2. Of those that a mesh axis runs over, the one named last changes fastest.
Arguments:
- activations: bfloat16 [4096, 8192], P(('rep', 'ada')), parts along dimension 0, may hold values from -1.5 to 1.5
- out_grads: bfloat16 [4096, 1024], P(('rep', 'ada')), parts along dimension 0, may hold values from -6 to 6
- base_weight: bfloat16 [8192, 1024], P('ada'), may hold values from -0.1875 to 0.1875
- adapter_in: bfloat16 [32, 8192, 128], P(('rep', 'ada')), parts along dimension 0, may hold values from -0.125 to 0.125
- adapter_out: bfloat16 [32, 128, 1024], P(('rep', 'ada')), parts along dimension 0, may hold values from -0.1875 to 0.1875
- tenant_ids: int32 [4096], P(('rep', 'ada')), parts along dimension 0, may hold values from 0 to 15, as said below
- slot_of: int32 [32], P('rep'), parts along dimension 0, may hold values from 0 to 15, each once
- ranks: int32 [32], P('rep'), parts along dimension 0, may hold values from 16 to 128, as said below
Outputs:
- input_grads: bfloat16 [4096, 8192], P(('rep', 'ada')), parts along dimension 0
- grad_in: float32 [32, 8192, 128], P(('rep', 'ada')), parts along dimension 0
- grad_out: float32 [32, 128, 1024], P(('rep', 'ada')), parts along dimension 0
There are 2 independent parts, one for each index of `rep`. A program takes and returns all parts, laid end to end along the dimension named above; an argument that names none is the same for every part. Nothing has to cross between parts.
Inputs may be any that keep to these rules, and one draw needn't show every extreme that they name: `tenant_ids`: the 128 tokens of one device name one tenant at most 16 times; in every draw one tenant is named exactly 16 times by the tokens of every device. `slot_of`: each slot holds exactly one tenant. `ranks`: multiples of 16.
All inputs are finite; a program needn't handle non-finite values.
Results may differ from a plain program's by a relative error of at most 0.0034.
Values may be sent and summed in bfloat16 or wider, within the bound.
A program may use at most 128 MiB of HBM per device.

v0:
```python
import jax
import jax.numpy as jnp
from jax import lax
from jax.sharding import PartitionSpec as P


def base_term(out_grads, base_weight):
    return lax.dot_general(
        out_grads,
        lax.all_gather(base_weight, "ada", axis=0, tiled=True),
        (((1,), (1,)), ((), ())),
        preferred_element_type=jnp.float32,
    )


def adapter_part(activations, out_grads, adapter_in, adapter_out, tenant_ids, slot_of, ranks):
    peers = lax.axis_size("ada")
    local_rows = activations.shape[0]
    capacity = max(2, 2 * local_rows // peers)
    tenant_count = slot_of.shape[0]
    tenant_range = jnp.arange(tenant_count, dtype=jnp.int32)
    destination = jnp.sum(
        jnp.where(tenant_ids[:, None] == tenant_range[None, :], slot_of[None, :], 0), axis=1
    )
    onehot = (destination[:, None] == jnp.arange(peers, dtype=jnp.int32)[None, :]).astype(jnp.int32)
    running = jnp.cumsum(onehot, axis=0)
    position = jnp.sum(onehot * running, axis=1) - 1
    placed = destination * capacity + position
    selector = (placed[None, :] == jnp.arange(peers * capacity, dtype=jnp.int32)[:, None]).astype(
        jnp.bfloat16
    )
    send_x = jnp.dot(selector, activations, preferred_element_type=jnp.float32).astype(jnp.bfloat16)
    send_g = jnp.dot(selector, out_grads, preferred_element_type=jnp.float32).astype(jnp.bfloat16)
    recv_x, recv_g = (
        lax.all_to_all(send_x, "ada", split_axis=0, concat_axis=0, tiled=True),
        lax.all_to_all(send_g, "ada", split_axis=0, concat_axis=0, tiled=True),
    )
    owner_index = lax.axis_index("ada")
    own_rank = jnp.sum(jnp.where(slot_of == owner_index, ranks, 0))
    scale = 4.0 / jnp.sqrt(own_rank.astype(jnp.float32))
    keep = jnp.arange(adapter_in.shape[2], dtype=jnp.int32) < own_rank
    down = jnp.where(keep[None, :], adapter_in[0], jnp.zeros_like(adapter_in[0]))
    upper = jnp.where(keep[:, None], adapter_out[0], jnp.zeros_like(adapter_out[0]))
    projected = jnp.dot(recv_x, down, preferred_element_type=jnp.float32).astype(jnp.bfloat16)
    inner_grad = (
        scale
        * lax.dot_general(
            recv_g, upper, (((1,), (1,)), ((), ())), preferred_element_type=jnp.float32
        )
    ).astype(jnp.bfloat16)
    grad_out = scale * lax.dot_general(
        projected, recv_g, (((0,), (0,)), ((), ())), preferred_element_type=jnp.float32
    )
    grad_in = lax.dot_general(
        recv_x, inner_grad, (((0,), (0,)), ((), ())), preferred_element_type=jnp.float32
    )
    returned = lax.dot_general(
        inner_grad, down, (((1,), (1,)), ((), ())), preferred_element_type=jnp.float32
    ).astype(jnp.bfloat16)
    arrived = lax.all_to_all(returned, "ada", split_axis=0, concat_axis=0, tiled=True)
    adapter_term = lax.dot_general(
        selector, arrived, (((0,), (0,)), ((), ())), preferred_element_type=jnp.float32
    )
    return (adapter_term, grad_in[None], grad_out[None])


def shards(
    activations, out_grads, base_weight, adapter_in, adapter_out, tenant_ids, slot_of, ranks
):
    base = base_term(out_grads, base_weight)
    adapter_term, grad_in, grad_out = adapter_part(
        activations, out_grads, adapter_in, adapter_out, tenant_ids, slot_of, ranks
    )
    input_grads = (base + adapter_term).astype(jnp.bfloat16)
    return (input_grads, grad_in, grad_out)


def solution(mesh):
    placed = (
        P(("rep", "ada"), None),
        P(("rep", "ada"), None),
        P("ada", None),
        P(("rep", "ada"), None, None),
        P(("rep", "ada"), None, None),
        P(("rep", "ada")),
        P("rep"),
        P("rep"),
    )
    return jax.shard_map(
        shards,
        mesh=mesh,
        in_specs=placed,
        out_specs=(
            P(("rep", "ada"), None),
            P(("rep", "ada"), None, None),
            P(("rep", "ada"), None, None),
        ),
        check_vma=False,
    )
```

profile of v0, /device:TPU:11, one launch (start us, length us, event | category | flops | bytes accessed | tf_op | source)
XLA Modules:
  0.0 332.2 jit_solution(10974653135685785817)
XLA Ops:
  7.2 0.0 copy-start
  7.2 0.0 all-gather.2.cloned.1.call-start
  7.2 0.7 all-gather.2.cloned.1.call-update
  7.9 0.8 select_reduce_fusion.1
  8.8 0.1 fusion.22
  8.9 0.2 reduce_window_sum.11
  9.0 0.2 select_reduce_fusion
  9.2 2.0 convolution_convert_fusion.2
  11.3 6.6 %all-to-all-start = ((bf16[16,16,1024]{2,1,0:T(8,128)(2,1)}), bf16[16,16,1024]{2,1,0:T(8,128)(2,1)S(1)}, u32[]{:S(2)}, u32[]{:S(2)}) async-start(bf16[16,16,1024]{2,1,0:T(8,128)(2,1)} %bitcast), calls=%async_computation | async-start | bytes 1048576 | tf_op jit(solution)/shard_map/all_to_all | solution.py:36
  17.8 3.3 convolution_convert_fusion
  21.1 22.4 %all-to-all-done = bf16[16,16,1024]{2,1,0:T(8,128)(2,1)S(1)} async-done(((bf16[16,16,1024]{2,1,0:T(8,128)(2,1)}), bf16[16,16,1024]{2,1,0:T(8,128)(2,1)S(1)}, u32[]{:S(2)}, u32[]{:S(2)}) %all-to-all-start) | async-done | bytes 524320 | tf_op jit(solution)/shard_map/all_to_all | solution.py:36
  43.5 6.3 %all-to-all-start.2 = ((bf16[16,16,8192]{2,1,0:T(8,128)(2,1)}), bf16[16,16,8192]{2,1,0:T(8,128)(2,1)}, u32[]{:S(2)}, u32[]{:S(2)}) async-start(bf16[16,16,8192]{2,1,0:T(8,128)(2,1)} %bitcast.34), calls=%async_computation.2 | async-start | bytes 8388608 | tf_op jit(solution)/shard_map/all_to_all | solution.py:35
  49.8 0.0 copy-done.2
  49.8 0.6 fusion.23
  51.2 0.7 iota_compare_fusion.6
  51.8 0.4 fusion.7
  52.2 4.8 %convolution_convert_fusion.1 = bf16[256,8192]{1,0:T(8,128)(2,1)} fusion(bf16[256,128]{1,0:T(8,128)(2,1)S(1)} %fusion.7, bf16[1,8192,128]{2,1,0:T(8,128)(2,1)} %param.11, pred[128]{0:T(512)(128)(4,1)S(1)} %iota_compare_fusion.6), kind=kOutput, calls=%fused_computation.1 | convolution fusion | flops 540016640 | bytes 6357120 | tf_op jit(solution)/shard_map/dot_general | solution.py:57
  57.0 166.1 %all-to-all-done.2 = bf16[16,16,8192]{2,1,0:T(8,128)(2,1)} async-done(((bf16[16,16,8192]{2,1,0:T(8,128)(2,1)}), bf16[16,16,8192]{2,1,0:T(8,128)(2,1)}, u32[]{:S(2)}, u32[]{:S(2)}) %all-to-all-start.2) | async-done | bytes 4194336 | tf_op jit(solution)/shard_map/all_to_all | solution.py:35
  223.1 4.4 %all-to-all-start.1 = ((bf16[16,16,8192]{2,1,0:T(8,128)(2,1)}), bf16[16,16,8192]{2,1,0:T(8,128)(2,1)}, u32[]{:S(2)}, u32[]{:S(2)}) async-start(bf16[16,16,8192]{2,1,0:T(8,128)(2,1)} %bitcast.35), calls=%async_computation.1 | async-start | bytes 8388608 | tf_op jit(solution)/shard_map/all_to_all | solution.py:60
  227.5 5.5 %convolution_bitcast_fusion = f32[1,8192,128]{2,1,0:T(8,128)} fusion(bf16[256,8192]{1,0:T(8,128)(2,1)} %bitcast.7, bf16[256,128]{1,0:T(8,128)(2,1)S(1)} %fusion.7), kind=kOutput, calls=%fused_computation.2 | convolution fusion | flops 536870912 | bytes 8454144 | tf_op jit(solution)/shard_map/dot_general | solution.py:54
  233.1 5.2 %fusion.6 = f32[1,128,1024]{2,1,0:T(8,128)} fusion(bf16[256,1024]{1,0:T(8,128)(2,1)S(1)} %bitcast.37, bf16[256,8192]{1,0:T(8,128)(2,1)} %bitcast.7, bf16[1,8192,128]{2,1,0:T(8,128)(2,1)} %param.11, pred[128]{0:T(512)(128)(4,1)S(1)} %iota_compare_fusion.6, f32[]{:T(128)S(6)} %div.3), kind=kOutput, calls=%fused_computation.13 | convolution fusion | flops 605192192 | bytes 7340164 | tf_op jit(solution)/shard_map/dot_general | solution.py:51
  238.3 13.3 %fusion.28 = f32[128,8192]{1,0:T(8,128)} fusion(bf16[128,1024]{1,0:T(8,128)(2,1)S(1)} %copy-done.1, bf16[8192,1024]{1,0:T(8,128)(2,1)} %all-gather.2.cloned.1.call-done), kind=kOutput, calls=%fused_computation.39 | convolution fusion | flops 2147483648 | bytes 21233664 | tf_op jit(solution)/shard_map/dot_general | solution.py:8
  251.5 68.3 %all-to-all-done.1 = bf16[16,16,8192]{2,1,0:T(8,128)(2,1)} async-done(((bf16[16,16,8192]{2,1,0:T(8,128)(2,1)}), bf16[16,16,8192]{2,1,0:T(8,128)(2,1)}, u32[]{:S(2)}, u32[]{:S(2)}) %all-to-all-start.1) | async-done | bytes 4194336 | tf_op jit(solution)/shard_map/all_to_all | solution.py:60
  319.8 5.6 %fusion = bf16[128,8192]{1,0:T(8,128)(2,1)} fusion(f32[128,8192]{1,0:T(8,128)} %fusion.28, bf16[256,8192]{1,0:T(8,128)(2,1)} %bitcast.5, s32[128]{0:T(128)S(1)} %add_add_fusion), kind=kOutput, calls=%fused_computation.4 | convolution fusion | flops 539000832 | bytes 10486272 | tf_op jit(solution)/shard_map/dot_general | solution.py:61
  (10 shorter events, 0.0 us)
Async XLA Ops:
  7.2 10.7 %copy-start = (bf16[128,8192]{1,0:T(8,128)(2,1)S(1)}, bf16[128,8192]{1,0:T(8,128)(2,1)}, u32[]{:S(2)}) copy-start(bf16[128,8192]{1,0:T(8,128)(2,1)} %param.8) | copy-start | bytes 6291460
  7.2 231.1 %all-gather.2.cloned.1.call-start = ((), (), s32[]{:S(2)}) async-start(), calls=%async_computation.3 | async-start | bytes 17825792 | tf_op jit(solution)/shard_map/all_gather | solution.py:10
  11.3 32.3 %all-to-all-start = ((bf16[16,16,1024]{2,1,0:T(8,128)(2,1)}), bf16[16,16,1024]{2,1,0:T(8,128)(2,1)S(1)}, u32[]{:S(2)}, u32[]{:S(2)}) async-start(bf16[16,16,1024]{2,1,0:T(8,128)(2,1)} %bitcast), calls=%async_computation | async-start | bytes 1048576 | tf_op jit(solution)/shard_map/all_to_all | solution.py:36
  43.5 6.3 %copy-start.2 = (s32[16]{0:T(128)S(1)}, s32[16]{0:T(128)}, u32[]{:S(2)}) copy-start(s32[16]{0:T(128)} %param.14) | copy-start | bytes 196
  43.5 6.3 %copy-start.3 = (s32[16]{0:T(128)S(1)}, s32[16]{0:T(128)}, u32[]{:S(2)}) copy-start(s32[16]{0:T(128)} %param.15) | copy-start | bytes 196
  43.5 8.3 %copy-start.4 = (bf16[1,128,1024]{2,1,0:T(8,128)(2,1)S(1)}, bf16[1,128,1024]{2,1,0:T(8,128)(2,1)}, u32[]{:S(2)}) copy-start(bf16[1,128,1024]{2,1,0:T(8,128)(2,1)} %param.12) | copy-start | bytes 786436
  43.5 179.6 %all-to-all-start.2 = ((bf16[16,16,8192]{2,1,0:T(8,128)(2,1)}), bf16[16,16,8192]{2,1,0:T(8,128)(2,1)}, u32[]{:S(2)}, u32[]{:S(2)}) async-start(bf16[16,16,8192]{2,1,0:T(8,128)(2,1)} %bitcast.34), calls=%async_computation.2 | async-start | bytes 8388608 | tf_op jit(solution)/shard_map/all_to_all | solution.py:35
  223.1 96.7 %all-to-all-start.1 = ((bf16[16,16,8192]{2,1,0:T(8,128)(2,1)}), bf16[16,16,8192]{2,1,0:T(8,128)(2,1)}, u32[]{:S(2)}, u32[]{:S(2)}) async-start(bf16[16,16,8192]{2,1,0:T(8,128)(2,1)} %bitcast.35), calls=%async_computation.1 | async-start | bytes 8388608 | tf_op jit(solution)/shard_map/all_to_all | solution.py:60
  233.1 5.2 %copy-start.1 = (bf16[128,1024]{1,0:T(8,128)(2,1)S(1)}, bf16[128,1024]{1,0:T(8,128)(2,1)}, u32[]{:S(2)}) copy-start(bf16[128,1024]{1,0:T(8,128)(2,1)} %param.9) | copy-start | bytes 786436
Sparse Core Ops, SparseCore 0:
  10.2 210.8 all-gather.1
where the time goes:
time: 333 us; the launch traced here: 332 us
  waiting for transfers between devices  257 us (77%)
  matrix products  40 us (12%)
  starting transfers between devices  17.3 us (5%)
  between operations  14.8 us (4%)
    all_to_all x1, waiting for transfers between devices, adapter_part(): lax.all_to_all(send_x, 'ada', split_axis=0, concat_axis=0, tiled=True)  166 us
    all_to_all x1, waiting for transfers between devices, adapter_part(): lax.all_to_all(returned, 'ada', split_axis=0, concat_axis=0, tiled=True)  68.3 us
    all_to_all x1, waiting for transfers between devices, adapter_part(): lax.all_to_all(send_g, 'ada', split_axis=0, concat_axis=0, tiled=True)  22.4 us
    dot_general x1, matrix products, base_term(): lax.dot_general(out_grads, lax.all_gather(base_weight, 'ada', axis=0, til...  13.3 us
  transfers between devices with their start and end apart: 4, of which 3 were waited for; matrix products, arithmetic and copies ran while one was open for 11% of the time, Pallas kernels for 0%

commit v1 on v0

--- a/solution.py
+++ b/solution.py
@@ -1,7 +1,374 @@
+import functools
+
 import jax
 import jax.numpy as jnp
 from jax import lax
+from jax.experimental import pallas as pl
+from jax.experimental.pallas import tpu as pltpu
 from jax.sharding import PartitionSpec as P
+
+MESH = pl.DeviceIdType.MESH
+NT = (((1,), (1,)), ((), ()))
+TN = (((0,), (0,)), ((), ()))
+LANES = 128
+F32 = jnp.float32
+BF16 = jnp.bfloat16
+
+
+def dot_f32(a, b, dims):
+    return lax.dot_general(a, b, dims, preferred_element_type=F32)
+
+
+def kernel(
+    n, parts,
+    x_ref, gb_ref, w_ref, a_ref, place_ref, cmask_ref, own_ref,
+    out_ref, gin_ref, gout_ref,
+    gball, pall, acat, xsel, xrecv, ret, inner, tslot, rg, gin, gout,
+    g_recv, g_send, p_recv, p_send, a_recv, a_send, x_recv, x_send, r_recv, r_send,
+    local_sem, gin_sem, gout_sem, ownret_sem,
+):
+    me = lax.axis_index("ada")
+    z, lane = me // 4, me % 4
+    xx, core = lane // 2, lane % 2
+    nz = n // 4
+    rows = gb_ref.shape[1]
+    dim = x_ref.shape[1]
+    cols = dim // n
+    width = dim // parts
+    cap = xsel.shape[1] // n
+    step = 512
+
+    def index(zo, xo, co):
+        return zo * 4 + xo * 2 + co
+
+    def remote(src, dst, send, recv, target):
+        return pltpu.make_async_remote_copy(
+            src_ref=src, dst_ref=dst, send_sem=send, recv_sem=recv,
+            device_id={"ada": target}, device_id_type=MESH,
+        )
+
+    barrier = pltpu.get_barrier_semaphore()
+    for k in range(1, n):
+        pl.semaphore_signal(
+            barrier, inc=1, device_id={"ada": (me + k) % n}, device_id_type=MESH
+        )
+    pl.semaphore_wait(barrier, n - 1)
+
+    def block(o):
+        return gball.at[:, pl.ds(pl.multiple_of(o * rows, rows), rows), :]
+
+    def gcopy(kind, o, target, first=False):
+        return remote(
+            gb_ref if first else block(o), block(o), g_send.at[kind, o], g_recv.at[o], target
+        )
+
+    def wait_g(o):
+        gcopy(0, o, (me + 1) % n).wait_recv()
+
+    other_x = index(z, 1 - xx, core)
+    other_core = index(z, xx, 1 - core)
+    above = (me + 4) % n
+    below = (me + n - 4) % n
+
+    def z_up(o, first=False):
+        @pl.when(z < nz - 1)
+        def _():
+            gcopy(0, o, above, first).start()
+
+    def z_down(o, first=False):
+        @pl.when(z > 0)
+        def _():
+            gcopy(1, o, below, first).start()
+
+    z_up(me, True)
+    z_down(me, True)
+    gcopy(2, me, other_x, True).start()
+    gcopy(3, me, other_core, True).start()
+    own_gb = pltpu.make_async_copy(gb_ref, block(me), local_sem.at[0])
+    own_gb.start()
+
+    def pcopy(k):
+        target = (me + k) % n
+        return remote(place_ref, pall.at[me], p_send.at[k], p_recv.at[me], target)
+
+    for k in range(1, n):
+        pcopy(k).start()
+    own_p = pltpu.make_async_copy(place_ref, pall.at[me], local_sem.at[1])
+    own_p.start()
+
+    def acopy(k):
+        target = (me + k) % n
+        return remote(
+            a_ref.at[pl.ds(pl.multiple_of(target * cols, cols), cols), :],
+            acat.at[:, pl.ds(pl.multiple_of(me * LANES, LANES), LANES)],
+            a_send.at[k], a_recv.at[me], target,
+        )
+
+    for k in range(1, n):
+        acopy(k).start()
+    own_a = pltpu.make_async_copy(
+        a_ref.at[pl.ds(pl.multiple_of(me * cols, cols), cols), :],
+        acat.at[:, pl.ds(pl.multiple_of(me * LANES, LANES), LANES)],
+        local_sem.at[2],
+    )
+    own_a.start()
+
+    placed = place_ref[1:2, :]
+    pick = (
+        lax.broadcasted_iota(jnp.int32, (n * cap, rows), 0) == placed
+    ).astype(F32).astype(BF16)
+    for q in range(parts):
+        @pl.loop(0, width // step)
+        def _(i):
+            to = pl.ds(pl.multiple_of(i * step, step), step)
+            at = pl.ds(pl.multiple_of(q * width + i * step, step), step)
+            xsel[q, :, to] = jnp.dot(
+                pick, x_ref[:, at], preferred_element_type=F32
+            ).astype(BF16)
+
+    own_gb.wait()
+    for k in range(1, nz):
+        @pl.when(z - k >= 0)
+        def _():
+            o = me - 4 * k
+            wait_g(o)
+            z_up(o)
+            gcopy(2, o, other_x).start()
+            gcopy(3, o, other_core).start()
+
+        @pl.when(z + k < nz)
+        def _():
+            o = me + 4 * k
+            wait_g(o)
+            z_down(o)
+            gcopy(2, o, other_x).start()
+            gcopy(3, o, other_core).start()
+    for zo in range(nz):
+        o = index((z + zo) % nz, 1 - xx, core)
+        wait_g(o)
+        gcopy(3, o, other_core).start()
+
+    def xcopy(q, k):
+        target = (me + k) % n
+        return remote(
+            xsel.at[q, pl.ds(pl.multiple_of(target * cap, cap), cap), :],
+            xrecv.at[q, pl.ds(pl.multiple_of(me * cap, cap), cap), :],
+            x_send.at[q, k], x_recv.at[q, me], target,
+        )
+
+    own_x = []
+    for q in range(parts):
+        for k in range(1, n):
+            xcopy(q, k).start()
+        own_x.append(pltpu.make_async_copy(
+            xsel.at[q, pl.ds(pl.multiple_of(me * cap, cap), cap), :],
+            xrecv.at[q, pl.ds(pl.multiple_of(me * cap, cap), cap), :],
+            local_sem.at[4 + q],
+        ))
+        own_x[-1].start()
+
+    for zo in range(nz):
+        for xo in range(2):
+            wait_g(index((z + zo) % nz, xo, 1 - core))
+    own_p.wait()
+    for k in range(1, n):
+        o = (me + k) % n
+        remote(place_ref, pall.at[o], p_send.at[k], p_recv.at[o], o).wait_recv()
+
+    @pl.loop(0, n)
+    def _(d):
+        at = pl.ds(pl.multiple_of(d * rows, rows), rows)
+        tslot[at, :] = jnp.broadcast_to(pall[d, 0:1, :], (rows, LANES)).T
+        mine = (
+            lax.broadcasted_iota(jnp.int32, (cap, rows), 0) + me * cap == pall[d, 1:2, :]
+        ).astype(F32).astype(BF16)
+        rg[pl.ds(pl.multiple_of(d * cap, cap), cap), :] = jnp.dot(
+            mine, gball[0, at, :], preferred_element_type=F32
+        ).astype(BF16)
+
+    scaled_keep, keep, scale = own_ref[0:1, :], own_ref[1:2, :], own_ref[2:3, 0:1]
+    ig = (scaled_keep * dot_f32(rg[...], gb_ref[1], NT)).astype(BF16)
+
+    own_a.wait()
+    for k in range(1, n):
+        o = (me + k) % n
+        remote(
+            a_ref.at[pl.ds(0, cols), :],
+            acat.at[:, pl.ds(pl.multiple_of(o * LANES, LANES), LANES)],
+            a_send.at[k], a_recv.at[o], o,
+        ).wait_recv()
+
+    quad = 4 * rows
+    slots_step = step // LANES
+
+    def rcopy(target):
+        return remote(
+            ret.at[pl.ds(pl.multiple_of(target * rows, rows), rows), :],
+            out_ref.at[:, pl.ds(pl.multiple_of(me * cols, cols), cols)],
+            r_send.at[target], r_recv.at[me], target,
+        )
+
+    own_ret = pltpu.make_async_copy(
+        ret.at[pl.ds(pl.multiple_of(me * rows, rows), rows), :],
+        out_ref.at[:, pl.ds(pl.multiple_of(me * cols, cols), cols)],
+        ownret_sem,
+    )
+
+    @pl.loop(0, nz)
+    def _(i):
+        zt = (z + 1 + i) % nz
+        at = pl.ds(pl.multiple_of(zt * quad, quad), quad)
+
+        @pl.loop(0, n * LANES // step)
+        def _(j):
+            to = pl.ds(pl.multiple_of(j * step, step), step)
+            acc = dot_f32(gball[0, at, :], gball[1, to, :], NT) * cmask_ref[0:1, to]
+            for s in range(slots_step):
+                hit = tslot[at, :] == j * slots_step + s
+                part = pl.ds(pl.multiple_of(j * step + s * LANES, LANES), LANES)
+                inner[:, part] = jnp.where(
+                    hit, acc[:, s * LANES:(s + 1) * LANES], 0.0
+                ).astype(BF16)
+
+        term = dot_f32(inner[...], acat[...], NT).astype(BF16).astype(F32)
+        ret[at, :] = (dot_f32(gball[0, at, :], w_ref[...], NT) + term).astype(BF16)
+        for t in range(4):
+            target = zt * 4 + t
+
+            @pl.when(target != me)
+            def _():
+                rcopy(target).start()
+
+            @pl.when(target == me)
+            def _():
+                own_ret.start()
+
+    proj = jnp.zeros((n * cap, LANES), F32)
+    for q in range(parts):
+        own_x[q].wait()
+        for k in range(1, n):
+            o = (me + k) % n
+            remote(
+                xsel.at[q, pl.ds(0, cap), :],
+                xrecv.at[q, pl.ds(pl.multiple_of(o * cap, cap), cap), :],
+                x_send.at[q, k], x_recv.at[q, o], o,
+            ).wait_recv()
+        proj += jnp.dot(
+            xrecv[q], a_ref[pl.ds(q * width, width), :], preferred_element_type=F32
+        )
+
+        @pl.loop(0, width // step)
+        def _(i):
+            at = pl.ds(pl.multiple_of(i * step, step), step)
+            gin[q, at, :] = dot_f32(xrecv[q, :, at], ig, TN)
+
+        pltpu.make_async_copy(
+            gin.at[q], gin_ref.at[pl.ds(q * width, width), :], gin_sem.at[q]
+        ).start()
+    projected = (proj * keep).astype(BF16)
+    gout[...] = scale * dot_f32(projected, rg[...], TN)
+    out_copy = pltpu.make_async_copy(gout, gout_ref, gout_sem)
+    out_copy.start()
+
+    own_ret.wait()
+    for k in range(1, n):
+        o = (me + k) % n
+        remote(
+            ret.at[pl.ds(0, rows), :],
+            out_ref.at[:, pl.ds(pl.multiple_of(o * cols, cols), cols)],
+            r_send.at[o], r_recv.at[o], o,
+        ).wait_recv()
+        rcopy(o).wait_send()
+        acopy(k).wait_send()
+        pcopy(k).wait_send()
+        for q in range(parts):
+            xcopy(q, k).wait_send()
+    for zo in range(nz):
+        o = index(zo, xx, core)
+        gcopy(2, o, other_x).wait_send()
+        gcopy(3, o, other_core).wait_send()
+        gcopy(3, index(zo, 1 - xx, core), other_core).wait_send()
+
+        @pl.when((zo <= z) & (z < nz - 1))
+        def _():
+            gcopy(0, o, above).wait_send()
+
+        @pl.when((zo >= z) & (z > 0))
+        def _():
+            gcopy(1, o, below).wait_send()
+    for q in range(parts):
+        pltpu.make_async_copy(
+            gin.at[q], gin_ref.at[pl.ds(q * width, width), :], gin_sem.at[q]
+        ).wait()
+    out_copy.wait()
+
+
+def routed(activations, out_grads, base_weight, adapter_in, adapter_out, tenant_ids, slot_of, ranks):
+    n = lax.axis_size("ada")
+    rows, dim = activations.shape
+    dk = out_grads.shape[1]
+    cap = max(2, 2 * rows // n)
+    cols = dim // n
+    parts = 4
+    tenants = jnp.arange(slot_of.shape[0], dtype=jnp.int32)
+    destination = jnp.sum(
+        jnp.where(tenant_ids[:, None] == tenants[None, :], slot_of[None, :], 0), axis=1
+    )
+    onehot = (destination[:, None] == tenants[None, :]).astype(jnp.int32)
+    earlier = jnp.arange(rows)[:, None] > jnp.arange(rows)[None, :]
+    same = destination[:, None] == destination[None, :]
+    position = jnp.sum((earlier & same).astype(jnp.int32), axis=1)
+    placed = destination * cap + position
+    place = jnp.zeros((8, rows), jnp.int32).at[0].set(destination).at[1].set(placed)
+    slot_rank = jnp.sum(jnp.where(slot_of[None, :] == tenants[:, None], ranks[None, :], 0), axis=1)
+    scale = 4.0 / jnp.sqrt(slot_rank.astype(F32))
+    keep = (jnp.arange(LANES, dtype=jnp.int32)[None, :] < slot_rank[:, None]).astype(F32)
+    cmask = (scale[:, None] * keep).reshape(1, -1)
+    mine = tenants == lax.axis_index("ada")
+    own_scale = jnp.sum(jnp.where(mine, scale, 0.0))
+    own_keep = jnp.sum(jnp.where(mine[:, None], keep, 0.0), axis=0)
+    own = jnp.stack([own_scale * own_keep, own_keep, jnp.full((LANES,), own_scale)])
+    own = jnp.pad(own, ((0, 5), (0, 0)))
+    gb = jnp.stack([out_grads, adapter_out[0]])
+    vmem = pl.BlockSpec(memory_space=pltpu.VMEM)
+    any_space = pl.BlockSpec(memory_space=pl.ANY)
+    dma = pltpu.SemaphoreType.DMA
+    input_grads, grad_in, grad_out = pl.pallas_call(
+        functools.partial(kernel, n, parts),
+        out_shape=(
+            jax.ShapeDtypeStruct((rows, dim), BF16),
+            jax.ShapeDtypeStruct((dim, LANES), F32),
+            jax.ShapeDtypeStruct((LANES, dk), F32),
+        ),
+        in_specs=[vmem] * 7,
+        out_specs=(any_space,) * 3,
+        scratch_shapes=[
+            pltpu.VMEM((2, n * rows, dk), BF16),
+            pltpu.VMEM((n, 8, rows), jnp.int32),
+            pltpu.VMEM((cols, n * LANES), BF16),
+            pltpu.VMEM((parts, n * cap, dim // parts), BF16),
+            pltpu.VMEM((parts, n * cap, dim // parts), BF16),
+            pltpu.VMEM((n * rows, cols), BF16),
+            pltpu.VMEM((4 * rows, n * LANES), BF16),
+            pltpu.VMEM((n * rows, LANES), jnp.int32),
+            pltpu.VMEM((n * cap, dk), BF16),
+            pltpu.VMEM((parts, dim // parts, LANES), F32),
+            pltpu.VMEM((LANES, dk), F32),
+            dma((n,)), dma((4, n)),
+            dma((n,)), dma((n,)),
+            dma((n,)), dma((n,)),
+            dma((parts, n)), dma((parts, n)),
+            dma((n,)), dma((n,)),
+            dma((4 + parts,)), dma((parts,)), dma, dma,
+        ],
+        compiler_params=pltpu.CompilerParams(
+            collective_id=0, has_side_effects=True, vmem_limit_bytes=56 * 2**20
+        ),
+        cost_estimate=pl.CostEstimate(
+            flops=17 * 10**9, bytes_accessed=12 * 2**20, transcendentals=0
+        ),
+    )(activations, gb, base_weight, adapter_in[0], place, cmask, own)
+    return (input_grads, grad_in[None], grad_out[None])
 
 
 def base_term(out_grads, base_weight):
@@ -64,7 +431,7 @@
     return (adapter_term, grad_in[None], grad_out[None])
 
 
-def shards(
+def gathered(
     activations, out_grads, base_weight, adapter_in, adapter_out, tenant_ids, slot_of, ranks
 ):
     base = base_term(out_grads, base_weight)
@@ -73,6 +440,13 @@
     )
     input_grads = (base + adapter_term).astype(jnp.bfloat16)
     return (input_grads, grad_in, grad_out)
+
+
+def shards(activations, *rest):
+    n = lax.axis_size("ada")
+    rows, dim = activations.shape
+    whole = n % 4 == 0 and rows == LANES and (2 * rows // n) % 16 == 0 and dim % (512 * n) == 0
+    return (routed if whole else gathered)(activations, *rest)
 
 
 def solution(mesh):

time: 333 us -> 242 us (0.73)
  waiting for transfers between devices: 257 us -> 0 us
  Pallas kernels: 0 us -> 228 us
  matrix products: 40 us -> 0 us
  starting transfers between devices: 17.3 us -> 0 us
  between operations: 14.8 us -> 0.71 us
  local copies, waits for them, and re-layouts: 0.02 us -> 6.75 us
  other arithmetic: 2.56 us -> 6.13 us
    all_to_all x3 -> x0, waiting for transfers between devices: 257 us -> none  [the longest x1 166 us: adapter_part(): lax.all_to_all(send_x, 'ada', split_axis=0, concat_axis=0, tiled=True)]
    pallas_call x0 -> x1, Pallas kernels: none -> 228 us  [routed(): pl.pallas_call(functools.partial(kernel, n, parts), out_shape=(jax.ShapeD...]
    dot_general x8 -> x0, matrix products: 40 us -> none  [the longest x1 13.3 us: base_term(): lax.dot_general(out_grads, lax.all_gather(base_weight, 'ada', axis=0, til...]
    all_to_all x3 -> x0, starting transfers between devices: 17.3 us -> none  [the longest x1 6.55 us: adapter_part(): lax.all_to_all(send_g, 'ada', split_axis=0, concat_axis=0, tiled=True)]
    unnamed x10 -> x9, local copies, waits for them, and re-layouts: 0.02 us -> 6.07 us
  transfers between devices with their start and end apart: 4 -> 0, of which waited for: 3 -> 0; matrix products, arithmetic and copies ran while one was open for 11% -> 0% of each run, Pallas kernels for 0% -> 0%
where the time goes in v1:
time: 242 us
  Pallas kernels  228 us (94%)
  local copies, waits for them, and re-layouts  6.75 us (3%)
  other arithmetic  6.13 us (3%)
    pallas_call x1, Pallas kernels, routed(): pl.pallas_call(functools.partial(kernel, n, parts), out_shape=(jax.ShapeD...  228 us
    unnamed x9, local copies, waits for them, and re-layouts  6.07 us

profile of v1, /device:TPU:11, one launch (start us, length us, event | category | flops | bytes accessed | tf_op | source)
XLA Modules:
  0.0 242.0 jit_solution(17561766423680437321)
XLA Ops:
  0.6 0.8 select_reduce_fusion.2
  1.4 0.8 select_reduce_fusion.1
  2.2 0.2 convert_reduce_fusion
  2.4 0.6 select_reduce_fusion.3
  3.0 0.6 mul.39
  3.7 0.0 copy-start.2
  3.7 0.7 select_reduce_fusion
  4.4 0.6 broadcast_multiply_fusion
  5.0 0.6 select_maximum_fusion.own_ref
  5.6 1.9 pad_maximum_fusion.gb_ref
  7.5 0.0 copy-done.2
  7.5 228.4 %shard_map.103 = (bf16[128,8192]{1,0:T(8,128)(2,1)}, f32[8192,128]{1,0:T(8,128)}, f32[128,1024]{1,0:T(8,128)}) custom-call(bf16[128,8192]{1,0:T(8,128)(2,1)} %x_ref.1, bf16[2,128,1024]{2,1,0:T(8,128)(2,1)} %pad_maximum_fusion.gb_ref, bf16[512,1024]{1,0:T(8,128)(2,1)} %w_ref.1, bf16[8192,128]{1,0:T(8,128)(2,1)} %bitcast.17, s32[8,128]{1,0:T(8,128)} %copy-done.2, ...), custom_call_target="tpu_custom_call" | custom-call | flops 16999999488 | bytes 12582912 | tf_op jit(solution)/shard_map/pallas_call | solution.py:336
  235.9 0.0 copy-start
  235.9 3.2 %copy.15 = bf16[128,8192]{1,0:T(8,128)(2,1)} copy(bf16[128,8192]{1,0:T(8,128)(2,1)} %get-tuple-element.40) | data formatting | bytes 4194304
  239.2 0.0 copy-done
  239.2 0.0 copy-start.1
  239.2 2.0 copy.16
  241.2 0.0 copy-done.1
  241.2 0.8 copy.17
  (4 shorter events, 0.1 us)
Async XLA Ops:
  3.7 3.8 %copy-start.2 = (s32[8,128]{1,0:T(8,128)}, s32[8,128]{1,0:T(8,128)S(1)}, u32[]{:S(2)}) copy-start(s32[8,128]{1,0:T(8,128)S(1)} %scatter.9.place_ref) | copy-start | bytes 12292
  235.9 3.3 %copy-start = (f32[8192,128]{1,0:T(8,128)S(1)}, f32[8192,128]{1,0:T(8,128)}, u32[]{:S(2)}) copy-start(f32[8192,128]{1,0:T(8,128)} %get-tuple-element.31) | copy-start | bytes 12582916
  239.2 2.0 copy-start.1

commit v2 on v1

--- a/solution.py
+++ b/solution.py
@@ -20,18 +20,18 @@
 
 
 def kernel(
-    n, parts,
-    x_ref, gb_ref, w_ref, a_ref, place_ref, cmask_ref, own_ref,
+    n, parts, early,
+    x_ref, g_ref, b_ref, w_ref, a_ref, place_ref, own_ref,
     out_ref, gin_ref, gout_ref,
-    gball, pall, acat, xsel, xrecv, ret, inner, tslot, rg, gin, gout,
-    g_recv, g_send, p_recv, p_send, a_recv, a_send, x_recv, x_send, r_recv, r_send,
+    gall, iall, pall, acat, xsel, xrecv, ret, back, ig, rg, gin, gout,
+    g_recv, g_send, i_recv, i_send, p_recv, p_send, a_recv, a_send, x_recv, x_send, r_recv, r_send,
     local_sem, gin_sem, gout_sem, ownret_sem,
 ):
     me = lax.axis_index("ada")
     z, lane = me // 4, me % 4
     xx, core = lane // 2, lane % 2
     nz = n // 4
-    rows = gb_ref.shape[1]
+    rows = g_ref.shape[0]
     dim = x_ref.shape[1]
     cols = dim // n
     width = dim // parts
@@ -54,38 +54,91 @@
         )
     pl.semaphore_wait(barrier, n - 1)
 
-    def block(o):
-        return gball.at[:, pl.ds(pl.multiple_of(o * rows, rows), rows), :]
-
-    def gcopy(kind, o, target, first=False):
-        return remote(
-            gb_ref if first else block(o), block(o), g_send.at[kind, o], g_recv.at[o], target
-        )
-
-    def wait_g(o):
-        gcopy(0, o, (me + 1) % n).wait_recv()
-
     other_x = index(z, 1 - xx, core)
     other_core = index(z, xx, 1 - core)
     above = (me + 4) % n
     below = (me + n - 4) % n
 
-    def z_up(o, first=False):
-        @pl.when(z < nz - 1)
-        def _():
-            gcopy(0, o, above, first).start()
-
-    def z_down(o, first=False):
-        @pl.when(z > 0)
-        def _():
-            gcopy(1, o, below, first).start()
-
-    z_up(me, True)
-    z_down(me, True)
-    gcopy(2, me, other_x, True).start()
-    gcopy(3, me, other_core, True).start()
-    own_gb = pltpu.make_async_copy(gb_ref, block(me), local_sem.at[0])
-    own_gb.start()
+    def gather(own_ref, block, send_sem, recv_sem):
+        def copy(kind, o, target, first=False):
+            return remote(
+                own_ref if first else block(o), block(o), send_sem.at[kind, o], recv_sem.at[o],
+                target,
+            )
+
+        def wait(o):
+            copy(0, o, above).wait_recv()
+
+        def pass_on(o, first=False):
+            copy(2, o, other_x, first).start()
+            copy(3, o, other_core, first).start()
+
+        def up(o, first=False):
+            @pl.when(z < nz - 1)
+            def _():
+                copy(0, o, above, first).start()
+
+        def down(o, first=False):
+            @pl.when(z > 0)
+            def _():
+                copy(1, o, below, first).start()
+
+        def begin():
+            up(me, True)
+            down(me, True)
+            pass_on(me, True)
+
+        def relay(fill):
+            for k in range(1, nz):
+                @pl.when(z - k >= 0)
+                def _():
+                    wait(me - 4 * k)
+                    up(me - 4 * k)
+                    pass_on(me - 4 * k)
+
+                @pl.when(z + k < nz)
+                def _():
+                    wait(me + 4 * k)
+                    down(me + 4 * k)
+                    pass_on(me + 4 * k)
+
+                fill()
+            for zo in range(nz):
+                o = index((z + zo) % nz, 1 - xx, core)
+                wait(o)
+                copy(3, o, other_core).start()
+            fill()
+
+        def finish():
+            for zo in range(nz):
+                for xo in range(2):
+                    wait(index((z + zo) % nz, xo, 1 - core))
+
+        def drain():
+            for zo in range(nz):
+                o = index(zo, xx, core)
+                copy(2, o, other_x).wait_send()
+                copy(3, o, other_core).wait_send()
+                copy(3, index(zo, 1 - xx, core), other_core).wait_send()
+
+                @pl.when((zo <= z) & (z < nz - 1))
+                def _():
+                    copy(0, o, above).wait_send()
+
+                @pl.when((zo >= z) & (z > 0))
+                def _():
+                    copy(1, o, below).wait_send()
+
+        return begin, relay, finish, drain
+
+    def g_block(o):
+        return gall.at[pl.ds(pl.multiple_of(o * rows, rows), rows), :]
+
+    g_begin, g_relay, g_finish, g_drain = gather(g_ref, g_block, g_send, g_recv)
+    i_begin, i_relay, i_finish, i_drain = gather(ig, lambda o: iall.at[o], i_send, i_recv)
+    g_begin()
+    own_g = pltpu.make_async_copy(g_ref, g_block(me), local_sem.at[0])
+    own_g.start()
 
     def pcopy(k):
         target = (me + k) % n
@@ -104,8 +157,13 @@
             a_send.at[k], a_recv.at[me], target,
         )
 
-    for k in range(1, n):
-        acopy(k).start()
+    a_left = list(range(1, n))
+
+    def some_a():
+        for _ in range(min(len(a_left), n)):
+            acopy(a_left.pop(0)).start()
+
+    some_a()
     own_a = pltpu.make_async_copy(
         a_ref.at[pl.ds(pl.multiple_of(me * cols, cols), cols), :],
         acat.at[:, pl.ds(pl.multiple_of(me * LANES, LANES), LANES)],
@@ -126,27 +184,10 @@
                 pick, x_ref[:, at], preferred_element_type=F32
             ).astype(BF16)
 
-    own_gb.wait()
-    for k in range(1, nz):
-        @pl.when(z - k >= 0)
-        def _():
-            o = me - 4 * k
-            wait_g(o)
-            z_up(o)
-            gcopy(2, o, other_x).start()
-            gcopy(3, o, other_core).start()
-
-        @pl.when(z + k < nz)
-        def _():
-            o = me + 4 * k
-            wait_g(o)
-            z_down(o)
-            gcopy(2, o, other_x).start()
-            gcopy(3, o, other_core).start()
-    for zo in range(nz):
-        o = index((z + zo) % nz, 1 - xx, core)
-        wait_g(o)
-        gcopy(3, o, other_core).start()
+    own_g.wait()
+    g_relay(some_a)
+    while a_left:
+        some_a()
 
     def xcopy(q, k):
         target = (me + k) % n
@@ -157,7 +198,8 @@
         )
 
     own_x = []
-    for q in range(parts):
+
+    def send_x(q):
         for k in range(1, n):
             xcopy(q, k).start()
         own_x.append(pltpu.make_async_copy(
@@ -167,9 +209,15 @@
         ))
         own_x[-1].start()
 
-    for zo in range(nz):
-        for xo in range(2):
-            wait_g(index((z + zo) % nz, xo, 1 - core))
+    x_left = list(range(parts))
+
+    def some_x():
+        if x_left:
+            send_x(x_left.pop(0))
+
+    for _ in range(early):
+        some_x()
+    g_finish()
     own_p.wait()
     for k in range(1, n):
         o = (me + k) % n
@@ -177,17 +225,25 @@
 
     @pl.loop(0, n)
     def _(d):
-        at = pl.ds(pl.multiple_of(d * rows, rows), rows)
-        tslot[at, :] = jnp.broadcast_to(pall[d, 0:1, :], (rows, LANES)).T
         mine = (
             lax.broadcasted_iota(jnp.int32, (cap, rows), 0) + me * cap == pall[d, 1:2, :]
         ).astype(F32).astype(BF16)
         rg[pl.ds(pl.multiple_of(d * cap, cap), cap), :] = jnp.dot(
-            mine, gball[0, at, :], preferred_element_type=F32
+            mine, gall[pl.ds(pl.multiple_of(d * rows, rows), rows), :],
+            preferred_element_type=F32,
         ).astype(BF16)
 
     scaled_keep, keep, scale = own_ref[0:1, :], own_ref[1:2, :], own_ref[2:3, 0:1]
-    ig = (scaled_keep * dot_f32(rg[...], gb_ref[1], NT)).astype(BF16)
+    ig[...] = (scaled_keep * dot_f32(rg[...], b_ref[...], NT)).astype(BF16)
+    i_begin()
+    own_i = pltpu.make_async_copy(ig, iall.at[me], local_sem.at[3])
+    own_i.start()
+    own_i.wait()
+    some_x()
+    i_relay(some_x)
+    while x_left:
+        some_x()
+    i_finish()
 
     own_a.wait()
     for k in range(1, n):
@@ -199,7 +255,6 @@
         ).wait_recv()
 
     quad = 4 * rows
-    slots_step = step // LANES
 
     def rcopy(target):
         return remote(
@@ -214,24 +269,26 @@
         ownret_sem,
     )
 
+    @pl.loop(0, n)
+    def _(s):
+        down = acat[:, pl.ds(pl.multiple_of(s * LANES, LANES), LANES)]
+        term = dot_f32(iall[s], down, NT).astype(BF16)
+        back[:, pl.ds(pl.multiple_of(s * cap, cap), cap), :] = term.reshape(n, cap, cols)
+
     @pl.loop(0, nz)
     def _(i):
         zt = (z + 1 + i) % nz
         at = pl.ds(pl.multiple_of(zt * quad, quad), quad)
-
-        @pl.loop(0, n * LANES // step)
-        def _(j):
-            to = pl.ds(pl.multiple_of(j * step, step), step)
-            acc = dot_f32(gball[0, at, :], gball[1, to, :], NT) * cmask_ref[0:1, to]
-            for s in range(slots_step):
-                hit = tslot[at, :] == j * slots_step + s
-                part = pl.ds(pl.multiple_of(j * step + s * LANES, LANES), LANES)
-                inner[:, part] = jnp.where(
-                    hit, acc[:, s * LANES:(s + 1) * LANES], 0.0
-                ).astype(BF16)
-
-        term = dot_f32(inner[...], acat[...], NT).astype(BF16).astype(F32)
-        ret[at, :] = (dot_f32(gball[0, at, :], w_ref[...], NT) + term).astype(BF16)
+        base = dot_f32(gall[at, :], w_ref[...], NT)
+        for t in range(4):
+            d = zt * 4 + t
+            pick = (
+                lax.broadcasted_iota(jnp.int32, (n * cap, rows), 0) == pall[d, 1:2, :]
+            ).astype(F32).astype(BF16)
+            term = dot_f32(pick, back[d], TN)
+            ret[pl.ds(pl.multiple_of(d * rows, rows), rows), :] = (
+                base[t * rows:(t + 1) * rows] + term
+            ).astype(BF16)
         for t in range(4):
             target = zt * 4 + t
 
@@ -260,7 +317,7 @@
         @pl.loop(0, width // step)
         def _(i):
             at = pl.ds(pl.multiple_of(i * step, step), step)
-            gin[q, at, :] = dot_f32(xrecv[q, :, at], ig, TN)
+            gin[q, at, :] = dot_f32(xrecv[q, :, at], ig[...], TN)
 
         pltpu.make_async_copy(
             gin.at[q], gin_ref.at[pl.ds(q * width, width), :], gin_sem.at[q]
@@ -283,19 +340,8 @@
         pcopy(k).wait_send()
         for q in range(parts):
             xcopy(q, k).wait_send()
-    for zo in range(nz):
-        o = index(zo, xx, core)
-        gcopy(2, o, other_x).wait_send()
-        gcopy(3, o, other_core).wait_send()
-        gcopy(3, index(zo, 1 - xx, core), other_core).wait_send()
-
-        @pl.when((zo <= z) & (z < nz - 1))
-        def _():
-            gcopy(0, o, above).wait_send()
-
-        @pl.when((zo >= z) & (z > 0))
-        def _():
-            gcopy(1, o, below).wait_send()
+    g_drain()
+    i_drain()
     for q in range(parts):
         pltpu.make_async_copy(
             gin.at[q], gin_ref.at[pl.ds(q * width, width), :], gin_sem.at[q]
@@ -309,12 +355,11 @@
     dk = out_grads.shape[1]
     cap = max(2, 2 * rows // n)
     cols = dim // n
-    parts = 4
+    parts = 8
     tenants = jnp.arange(slot_of.shape[0], dtype=jnp.int32)
     destination = jnp.sum(
         jnp.where(tenant_ids[:, None] == tenants[None, :], slot_of[None, :], 0), axis=1
     )
-    onehot = (destination[:, None] == tenants[None, :]).astype(jnp.int32)
     earlier = jnp.arange(rows)[:, None] > jnp.arange(rows)[None, :]
     same = destination[:, None] == destination[None, :]
     position = jnp.sum((earlier & same).astype(jnp.int32), axis=1)
@@ -323,18 +368,16 @@
     slot_rank = jnp.sum(jnp.where(slot_of[None, :] == tenants[:, None], ranks[None, :], 0), axis=1)
     scale = 4.0 / jnp.sqrt(slot_rank.astype(F32))
     keep = (jnp.arange(LANES, dtype=jnp.int32)[None, :] < slot_rank[:, None]).astype(F32)
-    cmask = (scale[:, None] * keep).reshape(1, -1)
     mine = tenants == lax.axis_index("ada")
     own_scale = jnp.sum(jnp.where(mine, scale, 0.0))
     own_keep = jnp.sum(jnp.where(mine[:, None], keep, 0.0), axis=0)
     own = jnp.stack([own_scale * own_keep, own_keep, jnp.full((LANES,), own_scale)])
     own = jnp.pad(own, ((0, 5), (0, 0)))
-    gb = jnp.stack([out_grads, adapter_out[0]])
     vmem = pl.BlockSpec(memory_space=pltpu.VMEM)
     any_space = pl.BlockSpec(memory_space=pl.ANY)
     dma = pltpu.SemaphoreType.DMA
     input_grads, grad_in, grad_out = pl.pallas_call(
-        functools.partial(kernel, n, parts),
+        functools.partial(kernel, n, parts, 3),
         out_shape=(
             jax.ShapeDtypeStruct((rows, dim), BF16),
             jax.ShapeDtypeStruct((dim, LANES), F32),
@@ -343,17 +386,19 @@
         in_specs=[vmem] * 7,
         out_specs=(any_space,) * 3,
         scratch_shapes=[
-            pltpu.VMEM((2, n * rows, dk), BF16),
+            pltpu.VMEM((n * rows, dk), BF16),
+            pltpu.VMEM((n, n * cap, LANES), BF16),
             pltpu.VMEM((n, 8, rows), jnp.int32),
             pltpu.VMEM((cols, n * LANES), BF16),
             pltpu.VMEM((parts, n * cap, dim // parts), BF16),
             pltpu.VMEM((parts, n * cap, dim // parts), BF16),
             pltpu.VMEM((n * rows, cols), BF16),
-            pltpu.VMEM((4 * rows, n * LANES), BF16),
-            pltpu.VMEM((n * rows, LANES), jnp.int32),
+            pltpu.VMEM((n, n * cap, cols), BF16),
+            pltpu.VMEM((n * cap, LANES), BF16),
             pltpu.VMEM((n * cap, dk), BF16),
             pltpu.VMEM((parts, dim // parts, LANES), F32),
             pltpu.VMEM((LANES, dk), F32),
+            dma((n,)), dma((4, n)),
             dma((n,)), dma((4, n)),
             dma((n,)), dma((n,)),
             dma((n,)), dma((n,)),
@@ -365,9 +410,9 @@
             collective_id=0, has_side_effects=True, vmem_limit_bytes=56 * 2**20
         ),
         cost_estimate=pl.CostEstimate(
-            flops=17 * 10**9, bytes_accessed=12 * 2**20, transcendentals=0
+            flops=6 * 10**9, bytes_accessed=12 * 2**20, transcendentals=0
         ),
-    )(activations, gb, base_weight, adapter_in[0], place, cmask, own)
+    )(activations, out_grads, adapter_out[0], base_weight, adapter_in[0], place, own)
     return (input_grads, grad_in[None], grad_out[None])
 
 
@@ -445,7 +490,7 @@
 def shards(activations, *rest):
     n = lax.axis_size("ada")
     rows, dim = activations.shape
-    whole = n % 4 == 0 and rows == LANES and (2 * rows // n) % 16 == 0 and dim % (512 * n) == 0
+    whole = n % 4 == 0 and rows == LANES and (2 * rows // n) % 16 == 0 and dim % (512 * n) == 0 and n >= 8
     return (routed if whole else gathered)(activations, *rest)
 
 

time: 242 us -> 228 us (0.942)
  Pallas kernels: 228 us -> 216 us
  other arithmetic: 6.13 us -> 3.68 us
    pallas_call x1, Pallas kernels: 228 us -> 216 us  [routed(): pl.pallas_call(functools.partial(kernel, n, parts, 3), out_shape=(jax.Sha...]
where the time goes in v2:
time: 228 us
  Pallas kernels  216 us (95%)
  local copies, waits for them, and re-layouts  7.33 us (3%)
  other arithmetic  3.68 us (2%)
    pallas_call x1, Pallas kernels, routed(): pl.pallas_call(functools.partial(kernel, n, parts, 3), out_shape=(jax.Sha...  216 us
    unnamed x9, local copies, waits for them, and re-layouts  6.65 us

profile of v2, /device:TPU:11, one launch (start us, length us, event | category | flops | bytes accessed | tf_op | source)
XLA Modules:
  0.0 228.0 jit_solution(4794472627379857368)
XLA Ops:
  0.6 0.8 select_reduce_fusion.2
  1.4 0.8 select_reduce_fusion.1
  2.2 0.6 select_reduce_fusion.3
  2.8 0.1 select_reduce_fusion
  2.9 0.6 broadcast_multiply_fusion
  3.5 0.6 mul.26
  4.2 0.2 convert_reduce_fusion
  4.4 0.6 select_maximum_fusion.own_ref
  5.0 0.0 copy-start.2
  5.0 0.6 copy-done.2
  5.6 216.3 %shard_map.103 = (bf16[128,8192]{1,0:T(8,128)(2,1)}, f32[8192,128]{1,0:T(8,128)}, f32[128,1024]{1,0:T(8,128)}) custom-call(bf16[128,8192]{1,0:T(8,128)(2,1)} %x_ref.1, bf16[128,1024]{1,0:T(8,128)(2,1)} %g_ref.1, bf16[128,1024]{1,0:T(8,128)(2,1)} %bitcast.15, bf16[512,1024]{1,0:T(8,128)(2,1)} %w_ref.1, bf16[8192,128]{1,0:T(8,128)(2,1)} %bitcast.14, ...), custom_call_target="tpu_custom_call" | custom-call | flops 6000000000 | bytes 12582912 | tf_op jit(solution)/shard_map/pallas_call | solution.py:379
  221.9 0.0 copy-start
  221.9 3.2 %copy.15 = bf16[128,8192]{1,0:T(8,128)(2,1)} copy(bf16[128,8192]{1,0:T(8,128)(2,1)} %get-tuple-element.36) | data formatting | bytes 4194304
  225.2 0.0 copy-done
  225.2 0.0 copy-start.1
  225.2 2.0 copy.16
  227.2 0.0 copy-done.1
  227.2 0.8 copy.17
  (4 shorter events, 0.0 us)
Async XLA Ops:
  5.0 0.6 copy-start.2
  221.9 3.3 %copy-start = (f32[8192,128]{1,0:T(8,128)S(1)}, f32[8192,128]{1,0:T(8,128)}, u32[]{:S(2)}) copy-start(f32[8192,128]{1,0:T(8,128)} %get-tuple-element.31) | copy-start | bytes 12582916
  225.2 2.0 copy-start.1
